TPU v7x, 32 devices: a whole 2x2x4 slice. The times are simulated.
32 devices in a mesh: gx: 8 (over y, x, core), gy: 4 (over z).
Axes of the slice: x: 2, y: 2, z: 4, core: 2. Of those that a mesh axis runs over, the one named last changes fastest.
Arguments:
- base_state: float32 [8, 32, 2048], P(None, 'gx', 'gy'), may hold values from -6 to 6
- misfit_weight: float32 [8, 32, 2048], P(None, 'gx', 'gy'), may hold values from 0.5 to 2
- state_deltas: bfloat16 [8, 8, 32, 2048], P(None, None, 'gx', 'gy'), may hold values from -3 to 3
- delta_index: int32 [2, 8], replicated, may hold values from 0 to 7
- diag_block: float32 [2, 8, 8, 32, 2048], P(None, None, None, 'gx', 'gy'), may hold values from -2 to 24, as said below
- precond: float32 [8, 8, 32, 2048], P(None, None, 'gx', 'gy'), may hold values from -0.03 to 0.25, as said below
- face_coupling: float32 [2, 4, 8, 32, 2048], P(None, None, None, 'gx', 'gy'), may hold values from 0.2 to 1
- accumulation: float32 [8, 32, 2048], P(None, 'gx', 'gy'), may hold values from 0.5 to 2
- well_diag: float32 [512], P('gx'), may hold values from 1 to 4
- perf_well: int32 [8, 4, 128], P('gx', 'gy'), may hold values from 0 to 63
- perf_cell: int32 [8, 4, 128], P('gx', 'gy'), may hold values from 0 to 2047
- perf_coef: float32 [2, 2, 8, 8, 4, 128], P(None, None, None, 'gx', 'gy'), may hold values from -0.9 to 0.9
Outputs:
- adjoint: float32 [2, 8, 32, 2048], P(None, None, 'gx', 'gy')
Inputs may be any that keep to these rules, and one draw needn't show every extreme that they name: `diag_block`: each cell's block has a dominant diagonal: diagonal entries at least 8 times the largest off-diagonal magnitude. `precond`: diagonal entries between 0.15 and 0.25, the others within -0.03 to 0.03.
All inputs are finite; a program needn't handle non-finite values.
Results may differ from a plain program's by a relative error of at most 0.0003.
Values sent between devices are 32-bit elements; how exact they have to be, the bound alone decides.
A program may use at most 64 MiB of HBM per device.

v0:
```python
import jax
import jax.numpy as jnp
from jax import lax
from jax.sharding import PartitionSpec as P

SWEEPS = 4


def with_halo(cells, sides, width):
    for axis, dim in sides:
        count = lax.axis_size(axis)
        ends = count - 1
        head = lax.slice_in_dim(cells, 0, width, axis=dim)
        tail = lax.slice_in_dim(cells, cells.shape[dim] - width, cells.shape[dim], axis=dim)
        cells = jnp.concatenate(
            [
                lax.ppermute(tail, axis, [(i, (i + 1) % count) for i in range(ends)]),
                cells,
                lax.ppermute(head, axis, [((i + 1) % count, i) for i in range(ends)]),
            ],
            axis=dim,
        )
    return cells


def select_delta(state_deltas, chosen):
    count = state_deltas.shape[0]
    match = chosen[None, :] == jnp.arange(count, dtype=jnp.int32)[:, None]
    return jnp.sum(
        jnp.where(match[:, :, None, None], state_deltas.astype(jnp.float32), jnp.float32(0.0)),
        axis=0,
    )


def local(
    base_state,
    misfit_weight,
    state_deltas,
    delta_index,
    diag_block,
    precond,
    face_coupling,
    accumulation,
    well_diag,
    perf_well,
    perf_cell,
    perf_coef,
):
    high = lax.Precision.HIGHEST
    comps, rows_x, rows_y = base_state.shape
    nwells = well_diag.shape[0]
    steps_all = diag_block.shape[0]
    sweeps_all = SWEEPS
    cell_ids = perf_cell[0, 0]
    well_sel = (perf_well[0, 0][:, None] == jnp.arange(nwells, dtype=jnp.int32)[None, :]).astype(
        jnp.float32
    )
    states = []
    running = base_state
    for step_no in range(steps_all):
        running = running + select_delta(state_deltas, delta_index[step_no])
        states.append(running)
    results = [None] * steps_all
    for step_no in range(steps_all - 1, -1, -1):
        coupling = face_coupling[step_no]
        rims = with_halo(coupling, (("gx", 2), ("gy", 3)), 1)
        diag_now = diag_block[step_no]
        row_coef = perf_coef[step_no, 0, :, 0, 0, :]
        col_coef = perf_coef[step_no, 1, :, 0, 0, :]
        rhs = misfit_weight * states[step_no]
        if step_no < steps_all - 1:
            rhs = rhs + accumulation * results[step_no + 1]
        solution = jnp.zeros_like(rhs)
        residual = rhs
        for sweep in range(sweeps_all):
            search = jnp.einsum("ijxy,jxy->ixy", precond, residual, precision=high)
            well_flattened = search.reshape(comps, rows_x * rows_y)
            picked = well_flattened[:, cell_ids]
            weighted = jnp.sum(row_coef * picked, axis=0)
            well_tot = lax.psum(jnp.dot(weighted, well_sel, precision=high), "gy")
            padded_v = with_halo(search, (("gx", 1), ("gy", 2)), 1)
            total = rims[1, :, :-2, 1:-1] * padded_v[:, :-2, 1:-1]
            total = total + rims[0, :, 2:, 1:-1] * padded_v[:, 2:, 1:-1]
            total = total + rims[3, :, 1:-1, :-2] * padded_v[:, 1:-1, :-2]
            total = total + rims[2, :, 1:-1, 2:] * padded_v[:, 1:-1, 2:]
            diag_part = jnp.einsum("jixy,jxy->ixy", diag_now, search, precision=high)
            per_perf = jnp.dot(well_sel, well_tot / well_diag, precision=high)
            flattened = jnp.zeros((comps, rows_x * rows_y), jnp.float32)
            flattened = flattened.at[:, cell_ids].add(col_coef * per_perf[None, :])
            image = diag_part - total - flattened.reshape(comps, rows_x, rows_y)
            totals = lax.psum((jnp.sum(residual * image), jnp.sum(image * image)), ("gx", "gy"))
            step_len = totals[0] / totals[1]
            solution = solution + step_len * search
            residual = residual - step_len * image
        results[step_no] = solution
    return jnp.stack(results)


def solution(mesh):
    return jax.shard_map(
        local,
        mesh=mesh,
        in_specs=(
            P(None, "gx", "gy"),
            P(None, "gx", "gy"),
            P(None, None, "gx", "gy"),
            P(),
            P(None, None, None, "gx", "gy"),
            P(None, None, "gx", "gy"),
            P(None, None, None, "gx", "gy"),
            P(None, "gx", "gy"),
            P("gx"),
            P("gx", "gy", None),
            P("gx", "gy", None),
            P(None, None, None, "gx", "gy", None),
        ),
        out_specs=P(None, None, "gx", "gy"),
        check_vma=False,
    )
```

profile of v0, /device:TPU:0, one launch (start us, length us, event | category | flops | bytes accessed | tf_op | source)
XLA Modules:
  0.0 615.9 jit_solution(14276234920945925334)
XLA Ops:
  5.1 3.6 collective-permute-start.1
  9.6 3.9 collective-permute-start
  15.5 3.2 collective-permute-start.20
  21.3 12.1 %psum.168 = f32[64]{0:T(128)S(1)} all-reduce(f32[64]{0:T(128)S(1)} %convolution_bitcast_fusion.15), channel_id=1, replica_groups=mesh['gx'=8,'gy'=4] {'gy'}, use_global_device_ids=true, to_apply=%region_3.4 | all-reduce | flops 64 | bytes 512 | tf_op jit(solution)/shard_map/psum | solution.py:80
  41.0 4.5 collective-permute-start.5
  50.8 5.2 collective-permute-start.24
  59.4 42.9 %all-reduce.7 = (f32[]{:T(128)}, f32[]{:T(128)}) all-reduce(f32[]{:T(128)} %get-tuple-element.22, f32[]{:T(128)} %get-tuple-element.21), channel_id=1, replica_groups=mesh['gx'=8,'gy'=4] {'gx','gy'}, use_global_device_ids=true, to_apply=%region_6.7 | all-reduce | flops 2 | bytes 16 | tf_op jit(solution)/shard_map/psum | solution.py:91
  106.2 10.0 %psum.171 = f32[64]{0:T(128)S(1)} all-reduce(f32[64]{0:T(128)S(1)} %convolution_bitcast_fusion.13), channel_id=1, replica_groups=mesh['gx'=8,'gy'=4] {'gy'}, use_global_device_ids=true, to_apply=%region_10.11 | all-reduce | flops 64 | bytes 512 | tf_op jit(solution)/shard_map/psum | solution.py:80
  117.8 3.6 collective-permute-start.8
  126.5 5.1 collective-permute-start.10
  135.0 42.4 %all-reduce.6 = (f32[]{:T(128)}, f32[]{:T(128)}) all-reduce(f32[]{:T(128)} %get-tuple-element.20, f32[]{:T(128)} %get-tuple-element.19), channel_id=1, replica_groups=mesh['gx'=8,'gy'=4] {'gx','gy'}, use_global_device_ids=true, to_apply=%region_13.14 | all-reduce | flops 2 | bytes 16 | tf_op jit(solution)/shard_map/psum | solution.py:91
  180.8 10.0 %psum.174 = f32[64]{0:T(128)S(1)} all-reduce(f32[64]{0:T(128)S(1)} %convolution_bitcast_fusion.11), channel_id=1, replica_groups=mesh['gx'=8,'gy'=4] {'gy'}, use_global_device_ids=true, to_apply=%region_17.18 | all-reduce | flops 64 | bytes 512 | tf_op jit(solution)/shard_map/psum | solution.py:80
  200.5 5.2 collective-permute-start.14
  209.5 42.0 %all-reduce.5 = (f32[]{:T(128)}, f32[]{:T(128)}) all-reduce(f32[]{:T(128)} %get-tuple-element.18, f32[]{:T(128)} %get-tuple-element.17), channel_id=1, replica_groups=mesh['gx'=8,'gy'=4] {'gx','gy'}, use_global_device_ids=true, to_apply=%region_20.21 | all-reduce | flops 2 | bytes 16 | tf_op jit(solution)/shard_map/psum | solution.py:91
  257.2 10.0 %psum.177 = f32[64]{0:T(128)S(1)} all-reduce(f32[64]{0:T(128)S(1)} %convolution_bitcast_fusion.9), channel_id=1, replica_groups=mesh['gx'=8,'gy'=4] {'gy'}, use_global_device_ids=true, to_apply=%region_24.25 | all-reduce | flops 64 | bytes 512 | tf_op jit(solution)/shard_map/psum | solution.py:80
  276.9 5.2 collective-permute-start.18
  285.3 42.1 %all-reduce.4 = (f32[]{:T(128)}, f32[]{:T(128)}) all-reduce(f32[]{:T(128)} %get-tuple-element.16, f32[]{:T(128)} %get-tuple-element.15), channel_id=1, replica_groups=mesh['gx'=8,'gy'=4] {'gx','gy'}, use_global_device_ids=true, to_apply=%region_27.28 | all-reduce | flops 2 | bytes 16 | tf_op jit(solution)/shard_map/psum | solution.py:91
  330.3 10.0 %psum.180 = f32[64]{0:T(128)S(1)} all-reduce(f32[64]{0:T(128)S(1)} %convolution_bitcast_fusion.7), channel_id=1, replica_groups=mesh['gx'=8,'gy'=4] {'gy'}, use_global_device_ids=true, to_apply=%region_31.32 | all-reduce | flops 64 | bytes 512 | tf_op jit(solution)/shard_map/psum | solution.py:80
  341.9 3.0 collective-permute-start.21
  348.8 4.5 collective-permute-start.25
  357.0 42.6 %all-reduce.3 = (f32[]{:T(128)}, f32[]{:T(128)}) all-reduce(f32[]{:T(128)} %get-tuple-element.14, f32[]{:T(128)} %get-tuple-element.13), channel_id=1, replica_groups=mesh['gx'=8,'gy'=4] {'gx','gy'}, use_global_device_ids=true, to_apply=%region_34.35 | all-reduce | flops 2 | bytes 16 | tf_op jit(solution)/shard_map/psum | solution.py:91
  402.4 10.0 %psum.183 = f32[64]{0:T(128)S(1)} all-reduce(f32[64]{0:T(128)S(1)} %convolution_bitcast_fusion.5), channel_id=1, replica_groups=mesh['gx'=8,'gy'=4] {'gy'}, use_global_device_ids=true, to_apply=%region_38.39 | all-reduce | flops 64 | bytes 512 | tf_op jit(solution)/shard_map/psum | solution.py:80
  414.0 3.0 collective-permute-start.28
  420.1 4.5 collective-permute-start.30
  427.2 43.6 %all-reduce.2 = (f32[]{:T(128)}, f32[]{:T(128)}) all-reduce(f32[]{:T(128)} %get-tuple-element.12, f32[]{:T(128)} %get-tuple-element.11), channel_id=1, replica_groups=mesh['gx'=8,'gy'=4] {'gx','gy'}, use_global_device_ids=true, to_apply=%region_41.42 | all-reduce | flops 2 | bytes 16 | tf_op jit(solution)/shard_map/psum | solution.py:91
  473.5 10.0 %psum.186 = f32[64]{0:T(128)S(1)} all-reduce(f32[64]{0:T(128)S(1)} %convolution_bitcast_fusion.3), channel_id=1, replica_groups=mesh['gx'=8,'gy'=4] {'gy'}, use_global_device_ids=true, to_apply=%region_45.46 | all-reduce | flops 64 | bytes 512 | tf_op jit(solution)/shard_map/psum | solution.py:80
  485.1 3.0 collective-permute-start.32
  491.2 5.1 collective-permute-start.34
  499.1 43.0 %all-reduce.1 = (f32[]{:T(128)}, f32[]{:T(128)}) all-reduce(f32[]{:T(128)} %get-tuple-element.10, f32[]{:T(128)} %get-tuple-element.9), channel_id=1, replica_groups=mesh['gx'=8,'gy'=4] {'gx','gy'}, use_global_device_ids=true, to_apply=%region_48.49 | all-reduce | flops 2 | bytes 16 | tf_op jit(solution)/shard_map/psum | solution.py:91
  545.5 10.0 %psum.189 = f32[64]{0:T(128)S(1)} all-reduce(f32[64]{0:T(128)S(1)} %convolution_bitcast_fusion.1), channel_id=1, replica_groups=mesh['gx'=8,'gy'=4] {'gy'}, use_global_device_ids=true, to_apply=%region_52.53 | all-reduce | flops 64 | bytes 512 | tf_op jit(solution)/shard_map/psum | solution.py:80
  563.2 4.5 collective-permute-start.38
  570.3 43.6 %all-reduce = (f32[]{:T(128)}, f32[]{:T(128)}) all-reduce(f32[]{:T(128)} %get-tuple-element.8, f32[]{:T(128)} %get-tuple-element.7), channel_id=1, replica_groups=mesh['gx'=8,'gy'=4] {'gx','gy'}, use_global_device_ids=true, to_apply=%region_55.56 | all-reduce | flops 2 | bytes 16 | tf_op jit(solution)/shard_map/psum | solution.py:91
  (285 shorter events, 112.3 us)
Async XLA Ops:
  3.8 33.1 %collective-permute-start.3 = (f32[8,1,512]{2,1,0:T(1,128)}, f32[8,1,512]{2,1,0:T(1,128)}, u32[]{:S(2)}, u32[]{:S(2)}) collective-permute-start(f32[8,1,512]{2,1,0:T(1,128)} %get-tuple-element.96), channel_id=1, source_target_pairs={{4,0},{8,4},{12,8},{16,12},{20,16},{24,20},{28,24},{5,1},{9,5},{13... | collective-permute-start | bytes 49160 | tf_op jit(solution)/shard_map/ppermute | solution.py:19
  5.1 33.8 %collective-permute-start.1 = (f32[8,1,512]{2,1,0:T(1,128)}, f32[8,1,512]{2,1,0:T(1,128)}, u32[]{:S(2)}, u32[]{:S(2)}) collective-permute-start(f32[8,1,512]{2,1,0:T(1,128)} %get-tuple-element.95), channel_id=1, source_target_pairs={{0,4},{4,8},{8,12},{12,16},{16,20},{20,24},{24,28},{1,5},{5,9},{9,... | collective-permute-start | bytes 49160 | tf_op jit(solution)/shard_map/ppermute | solution.py:17
  9.6 31.5 %collective-permute-start = (f32[4,8,1,512]{3,2,1,0:T(1,128)}, f32[4,8,1,512]{3,2,1,0:T(1,128)S(1)}, u32[]{:S(2)}, u32[]{:S(2)}) collective-permute-start(f32[4,8,1,512]{3,2,1,0:T(1,128)} %get-tuple-element.64), channel_id=1, source_target_pairs={{0,4},{4,8},{8,12},{12,16},{16,20},{20,24},{24,28},{1,5},{5,9},{9,... | collective-permute-start | bytes 196616 | tf_op jit(solution)/shard_map/ppermute | solution.py:17
  13.4 32.2 %collective-permute-start.2 = (f32[4,8,1,512]{3,2,1,0:T(1,128)}, f32[4,8,1,512]{3,2,1,0:T(1,128)}, u32[]{:S(2)}, u32[]{:S(2)}) collective-permute-start(f32[4,8,1,512]{3,2,1,0:T(1,128)} %get-tuple-element.63), channel_id=1, source_target_pairs={{4,0},{8,4},{12,8},{16,12},{20,16},{24,20},{28,24},{5,1},{9,5},{13... | collective-permute-start | bytes 196616 | tf_op jit(solution)/shard_map/ppermute | solution.py:19
  15.5 33.0 %collective-permute-start.20 = (f32[4,8,1,512]{3,2,1,0:T(1,128)}, f32[4,8,1,512]{3,2,1,0:T(1,128)S(1)}, u32[]{:S(2)}, u32[]{:S(2)}) collective-permute-start(f32[4,8,1,512]{3,2,1,0:T(1,128)} %get-tuple-element.62), channel_id=1, source_target_pairs={{0,4},{4,8},{8,12},{12,16},{16,20},{20,24},{24,28},{1,5},{5,9},{9,... | collective-permute-start | bytes 196616 | tf_op jit(solution)/shard_map/ppermute | solution.py:17
  37.6 12.3 %collective-permute-start.22 = (f32[4,8,1,512]{3,2,1,0:T(1,128)S(1)}, f32[4,8,1,512]{3,2,1,0:T(1,128)S(1)}, u32[]{:S(2)}, u32[]{:S(2)}) collective-permute-start(f32[4,8,1,512]{3,2,1,0:T(1,128)S(1)} %copy-done.26), channel_id=1, source_target_pairs={{4,0},{8,4},{12,8},{16,12},{20,16},{24,20},{28,24},{5,1},{9,5},{13... | collective-permute-start | bytes 196616 | tf_op jit(solution)/shard_map/ppermute | solution.py:19
  39.7 16.3 %collective-permute-start.7 = (f32[8,6,1]{2,1,0:T(8,128)S(1)}, f32[8,6,1]{2,1,0:T(8,128)S(1)}, u32[]{:S(2)}, u32[]{:S(2)}) collective-permute-start(f32[8,6,1]{2,1,0:T(8,128)S(1)} %get-tuple-element.80), channel_id=1, source_target_pairs={{1,0},{2,1},{3,2},{5,4},{6,5},{7,6},{9,8},{10,9},{11,10},{13,12},{... | collective-permute-start | bytes 584 | tf_op jit(solution)/shard_map/ppermute | solution.py:19
  41.0 16.3 %collective-permute-start.5 = (f32[8,6,1]{2,1,0:T(8,128)S(1)}, f32[8,6,1]{2,1,0:T(8,128)S(1)}, u32[]{:S(2)}, u32[]{:S(2)}) collective-permute-start(f32[8,6,1]{2,1,0:T(8,128)S(1)} %get-tuple-element.79), channel_id=1, source_target_pairs={{0,1},{1,2},{2,3},{4,5},{5,6},{6,7},{8,9},{9,10},{10,11},{12,13},{... | collective-permute-start | bytes 584 | tf_op jit(solution)/shard_map/ppermute | solution.py:17
  46.5 10.8 %collective-permute-start.4 = (f32[4,8,6,1]{3,2,1,0:T(8,128)S(1)}, f32[4,8,6,1]{3,2,1,0:T(8,128)S(1)}, u32[]{:S(2)}, u32[]{:S(2)}) collective-permute-start(f32[4,8,6,1]{3,2,1,0:T(8,128)S(1)} %get-tuple-element.60), channel_id=1, source_target_pairs={{0,1},{1,2},{2,3},{4,5},{5,6},{6,7},{8,9},{9,10},{10,11},{12,13},{... | collective-permute-start | bytes 2312 | tf_op jit(solution)/shard_map/ppermute | solution.py:17
  48.5 8.8 %collective-permute-start.6 = (f32[4,8,6,1]{3,2,1,0:T(8,128)S(1)}, f32[4,8,6,1]{3,2,1,0:T(8,128)S(1)}, u32[]{:S(2)}, u32[]{:S(2)}) collective-permute-start(f32[4,8,6,1]{3,2,1,0:T(8,128)S(1)} %get-tuple-element.59), channel_id=1, source_target_pairs={{1,0},{2,1},{3,2},{5,4},{6,5},{7,6},{9,8},{10,9},{11,10},{13,12},{... | collective-permute-start | bytes 2312 | tf_op jit(solution)/shard_map/ppermute | solution.py:19
  50.8 302.5 %collective-permute-start.24 = (f32[4,8,6,1]{3,2,1,0:T(8,128)}, f32[4,8,6,1]{3,2,1,0:T(8,128)}, u32[]{:S(2)}, u32[]{:S(2)}) collective-permute-start(f32[4,8,6,1]{3,2,1,0:T(8,128)} %get-tuple-element.58), channel_id=1, source_target_pairs={{0,1},{1,2},{2,3},{4,5},{5,6},{6,7},{8,9},{9,10},{10,11},{12,13},{... | collective-permute-start | bytes 2312 | tf_op jit(solution)/shard_map/ppermute | solution.py:17
  56.0 297.4 %collective-permute-start.26 = (f32[4,8,6,1]{3,2,1,0:T(8,128)}, f32[4,8,6,1]{3,2,1,0:T(8,128)}, u32[]{:S(2)}, u32[]{:S(2)}) collective-permute-start(f32[4,8,6,1]{3,2,1,0:T(8,128)} %get-tuple-element.57), channel_id=1, source_target_pairs={{1,0},{2,1},{3,2},{5,4},{6,5},{7,6},{9,8},{10,9},{11,10},{13,12},{... | collective-permute-start | bytes 2312 | tf_op jit(solution)/shard_map/ppermute | solution.py:19
  116.4 7.4 %collective-permute-start.9 = (f32[8,1,512]{2,1,0:T(1,128)}, f32[8,1,512]{2,1,0:T(1,128)}, u32[]{:S(2)}, u32[]{:S(2)}) collective-permute-start(f32[8,1,512]{2,1,0:T(1,128)} %get-tuple-element.94), channel_id=1, source_target_pairs={{4,0},{8,4},{12,8},{16,12},{20,16},{24,20},{28,24},{5,1},{9,5},{13... | collective-permute-start | bytes 49160 | tf_op jit(solution)/shard_map/ppermute | solution.py:19
  117.8 6.1 collective-permute-start.8
  125.2 7.4 %collective-permute-start.11 = (f32[8,6,1]{2,1,0:T(8,128)}, f32[8,6,1]{2,1,0:T(8,128)}, u32[]{:S(2)}, u32[]{:S(2)}) collective-permute-start(f32[8,6,1]{2,1,0:T(8,128)} %get-tuple-element.78), channel_id=1, source_target_pairs={{1,0},{2,1},{3,2},{5,4},{6,5},{7,6},{9,8},{10,9},{11,10},{13,12},{... | collective-permute-start | bytes 584 | tf_op jit(solution)/shard_map/ppermute | solution.py:19
  126.5 6.6 %collective-permute-start.10 = (f32[8,6,1]{2,1,0:T(8,128)}, f32[8,6,1]{2,1,0:T(8,128)}, u32[]{:S(2)}, u32[]{:S(2)}) collective-permute-start(f32[8,6,1]{2,1,0:T(8,128)} %get-tuple-element.77), channel_id=1, source_target_pairs={{0,1},{1,2},{2,3},{4,5},{5,6},{6,7},{8,9},{9,10},{10,11},{12,13},{... | collective-permute-start | bytes 584 | tf_op jit(solution)/shard_map/ppermute | solution.py:17
  191.0 7.4 %collective-permute-start.13 = (f32[8,1,512]{2,1,0:T(1,128)}, f32[8,1,512]{2,1,0:T(1,128)S(1)}, u32[]{:S(2)}, u32[]{:S(2)}) collective-permute-start(f32[8,1,512]{2,1,0:T(1,128)} %get-tuple-element.92), channel_id=1, source_target_pairs={{4,0},{8,4},{12,8},{16,12},{20,16},{24,20},{28,24},{5,1},{9,5},{13... | collective-permute-start | bytes 49160 | tf_op jit(solution)/shard_map/ppermute | solution.py:19
  192.4 6.1 collective-permute-start.12
  199.2 7.4 %collective-permute-start.15 = (f32[8,6,1]{2,1,0:T(8,128)}, f32[8,6,1]{2,1,0:T(8,128)}, u32[]{:S(2)}, u32[]{:S(2)}) collective-permute-start(f32[8,6,1]{2,1,0:T(8,128)} %get-tuple-element.76), channel_id=1, source_target_pairs={{1,0},{2,1},{3,2},{5,4},{6,5},{7,6},{9,8},{10,9},{11,10},{13,12},{... | collective-permute-start | bytes 584 | tf_op jit(solution)/shard_map/ppermute | solution.py:19
  200.5 6.5 %collective-permute-start.14 = (f32[8,6,1]{2,1,0:T(8,128)}, f32[8,6,1]{2,1,0:T(8,128)}, u32[]{:S(2)}, u32[]{:S(2)}) collective-permute-start(f32[8,6,1]{2,1,0:T(8,128)} %get-tuple-element.75), channel_id=1, source_target_pairs={{0,1},{1,2},{2,3},{4,5},{5,6},{6,7},{8,9},{9,10},{10,11},{12,13},{... | collective-permute-start | bytes 584 | tf_op jit(solution)/shard_map/ppermute | solution.py:17
  267.4 7.4 %collective-permute-start.17 = (f32[8,1,512]{2,1,0:T(1,128)}, f32[8,1,512]{2,1,0:T(1,128)S(1)}, u32[]{:S(2)}, u32[]{:S(2)}) collective-permute-start(f32[8,1,512]{2,1,0:T(1,128)} %get-tuple-element.90), channel_id=1, source_target_pairs={{4,0},{8,4},{12,8},{16,12},{20,16},{24,20},{28,24},{5,1},{9,5},{13... | collective-permute-start | bytes 49160 | tf_op jit(solution)/shard_map/ppermute | solution.py:19
  268.8 6.1 collective-permute-start.16
  275.6 7.4 %collective-permute-start.19 = (f32[8,6,1]{2,1,0:T(8,128)}, f32[8,6,1]{2,1,0:T(8,128)}, u32[]{:S(2)}, u32[]{:S(2)}) collective-permute-start(f32[8,6,1]{2,1,0:T(8,128)} %get-tuple-element.74), channel_id=1, source_target_pairs={{1,0},{2,1},{3,2},{5,4},{6,5},{7,6},{9,8},{10,9},{11,10},{13,12},{... | collective-permute-start | bytes 584 | tf_op jit(solution)/shard_map/ppermute | solution.py:19
  276.9 6.5 %collective-permute-start.18 = (f32[8,6,1]{2,1,0:T(8,128)}, f32[8,6,1]{2,1,0:T(8,128)}, u32[]{:S(2)}, u32[]{:S(2)}) collective-permute-start(f32[8,6,1]{2,1,0:T(8,128)} %get-tuple-element.73), channel_id=1, source_target_pairs={{0,1},{1,2},{2,3},{4,5},{5,6},{6,7},{8,9},{9,10},{10,11},{12,13},{... | collective-permute-start | bytes 584 | tf_op jit(solution)/shard_map/ppermute | solution.py:17
  340.5 6.3 %collective-permute-start.23 = (f32[8,1,512]{2,1,0:T(1,128)S(1)}, f32[8,1,512]{2,1,0:T(1,128)S(1)}, u32[]{:S(2)}, u32[]{:S(2)}) collective-permute-start(f32[8,1,512]{2,1,0:T(1,128)S(1)} %get-tuple-element.88), channel_id=1, source_target_pairs={{4,0},{8,4},{12,8},{16,12},{20,16},{24,20},{28,24},{5,1},{9,5},{13... | collective-permute-start | bytes 49160 | tf_op jit(solution)/shard_map/ppermute | solution.py:19
  348.8 6.1 collective-permute-start.25
  418.8 6.2 collective-permute-start.31
  420.1 6.1 collective-permute-start.30
  489.9 6.7 %collective-permute-start.35 = (f32[8,6,1]{2,1,0:T(8,128)S(1)}, f32[8,6,1]{2,1,0:T(8,128)S(1)}, u32[]{:S(2)}, u32[]{:S(2)}) collective-permute-start(f32[8,6,1]{2,1,0:T(8,128)S(1)} %get-tuple-element.68), channel_id=1, source_target_pairs={{1,0},{2,1},{3,2},{5,4},{6,5},{7,6},{9,8},{10,9},{11,10},{13,12},{... | collective-permute-start | bytes 584 | tf_op jit(solution)/shard_map/ppermute | solution.py:19
  491.2 6.1 collective-permute-start.34
  561.9 6.2 collective-permute-start.39
  563.2 6.1 collective-permute-start.38
  (51 other events, 636.7 us)
where the time goes:
time: 619 us; the launch traced here: 616 us
  blocking collectives  425 us (69%)
  starting transfers between devices  105 us (17%)
  other arithmetic  41 us (7%)
  local copies, waits for them, and re-layouts  25.4 us (4%)
  between operations  11.6 us (2%)
    psum x8, blocking collectives, local(): lax.psum((jnp.sum(residual * image), jnp.sum(image * image)), ('gx', 'gy'))  342 us
    psum x8, blocking collectives, local(): well_tot = lax.psum(jnp.dot(weighted, well_sel, precision=high), 'gy')  82.4 us
    ppermute x20, starting transfers between devices, with_halo(): lax.ppermute(tail, axis, [(i, (i + 1) % count) for i in range(ends)])  78.4 us
    ppermute x20, starting transfers between devices, with_halo(): lax.ppermute(head, axis, [((i + 1) % count, i) for i in range(ends)])  26.3 us
    reduce_sum x8, other arithmetic, local(): jnp.sum(image * image)  14.2 us
  transfers between devices with their start and end apart: 40, of which 7 were waited for; matrix products, arithmetic and copies ran while one was open for 8% of the time, Pallas kernels for 0%

commit v1 on v0

v1 whole, which is shorter than its diff:
```python
import functools

import jax
import jax.numpy as jnp
from jax import lax
from jax.experimental import pallas as pl
from jax.experimental.pallas import tpu as pltpu
from jax.sharding import PartitionSpec as P

SWEEPS = 4
LANES = 128
MESH = pl.DeviceIdType.MESH


def split3(x):
    a = x.astype(jnp.bfloat16)
    rest = x - a.astype(jnp.float32)
    b = rest.astype(jnp.bfloat16)
    c = (rest - b.astype(jnp.float32)).astype(jnp.bfloat16)
    return jnp.concatenate([a, b, c], axis=0)


def exact_dot(x, sel, transposed=False):
    rows = x.shape[0]
    dims = (((1,), (1 if transposed else 0,)), ((), ()))
    out = lax.dot_general(split3(x), sel, dims, preferred_element_type=jnp.float32)
    return out[:rows] + out[rows : 2 * rows] + out[2 * rows :]


def kernel(
    ngx,
    ngy,
    comps,
    nx,
    nch,
    nwells,
    steps,
    base_hbm,
    weight_hbm,
    deltas_hbm,
    index_ref,
    diag_hbm,
    precond_hbm,
    face_hbm,
    accum_hbm,
    wdiag_ref,
    pwell_ref,
    pcell_ref,
    pcoef_ref,
    out_ref,
    base,
    weight,
    deltas,
    diag,
    precond,
    face,
    accum,
    acc,
    edge,
    xlo_out,
    xhi_out,
    ylo_out,
    yhi_out,
    xlo_in,
    xhi_in,
    ylo_in,
    yhi_in,
    gy_buf,
    gx_buf,
    load_sem,
    send_sem,
    xlo_sem,
    xhi_sem,
    ylo_sem,
    yhi_sem,
    gy_sem,
    gx_sem,
):
    rows = nx * nch
    cells = (comps, rows, LANES)
    flat = (comps * rows, LANES)
    rounds = steps * (SWEEPS + 1)
    mx = lax.axis_index("gx")
    my = lax.axis_index("gy")
    has_xlo, has_xhi = mx > 0, mx < ngx - 1
    has_ylo, has_yhi = my > 0, my < ngy - 1

    loads = []
    order = (
        (base_hbm, base),
        (weight_hbm, weight),
        (deltas_hbm, deltas),
        (precond_hbm, precond),
        (face_hbm, face),
        (diag_hbm, diag),
        (accum_hbm, accum),
    )
    for n, (src, dst) in enumerate(order):
        cp = pltpu.make_async_copy(src, dst, load_sem.at[n])
        cp.start()
        loads.append(cp)

    barrier = pltpu.get_barrier_semaphore()
    for d in range(1, ngx):
        pl.semaphore_signal(
            barrier, inc=1, device_id=(lax.rem(mx + d, ngx), my), device_id_type=MESH
        )
    for d in range(1, ngy):
        pl.semaphore_signal(
            barrier, inc=1, device_id=(mx, lax.rem(my + d, ngy)), device_id_type=MESH
        )

    @pl.when(jnp.logical_not(has_xlo))
    def _():
        xlo_in[...] = jnp.zeros_like(xlo_in)

    @pl.when(jnp.logical_not(has_xhi))
    def _():
        xhi_in[...] = jnp.zeros_like(xhi_in)

    @pl.when(jnp.logical_not(has_ylo))
    def _():
        ylo_in[...] = jnp.zeros_like(ylo_in)

    @pl.when(jnp.logical_not(has_yhi))
    def _():
        yhi_in[...] = jnp.zeros_like(yhi_in)

    pcell = pcell_ref[0]
    length_y = nch * LANES
    p_lane = lax.rem(pcell, LANES)
    p_row = lax.rem(lax.div(pcell, LANES), nch) * nx + lax.div(pcell, length_y)
    nperf = pcell.shape[-1]
    lane_sel = (
        (lax.broadcasted_iota(jnp.int32, (LANES, nperf), 0) == p_lane)
        .astype(jnp.float32)
        .astype(jnp.bfloat16)
    )
    row_mask = lax.broadcasted_iota(jnp.int32, (rows, nperf), 0) == p_row
    well_mask = lax.broadcasted_iota(jnp.int32, (LANES, nperf), 0) == pwell_ref[0]
    well_sel = well_mask.astype(jnp.float32).astype(jnp.bfloat16)
    lane_ids = lax.broadcasted_iota(jnp.int32, (1, rows, LANES), 2)
    row_ids = lax.broadcasted_iota(jnp.int32, (1, rows, LANES), 1)
    sub_ids = lax.broadcasted_iota(jnp.int32, (8, LANES), 0)
    x_ids = lax.rem(row_ids, nx)

    loads[0].wait()
    loads[1].wait()
    loads[2].wait()
    states = []
    running = base[...]
    for k in range(steps):
        picked = [
            deltas[index_ref[k, c], c].astype(jnp.float32)[None] for c in range(comps)
        ]
        running = running + jnp.concatenate(picked, axis=0)
        states.append(running)

    def spread(c_row):
        full = jnp.where(row_mask[None], c_row[:, None, :], jnp.float32(0.0))
        return full.reshape(comps * rows, nperf)

    def apply_precond(v):
        total = precond[:, 0] * v[0][None]
        for j in range(1, comps):
            total = total + precond[:, j] * v[j][None]
        return total

    def neighbour_copy(src, dst, sem_out, sem_in, target):
        return pltpu.make_async_remote_copy(
            src_ref=src,
            dst_ref=dst,
            send_sem=sem_out,
            recv_sem=sem_in,
            device_id=target,
            device_id_type=MESH,
        )

    def wait_bytes(ref, sem):
        pltpu.make_async_copy(ref, ref, sem).wait()

    def operator(k, rnd, v, row_w, col_w, dots):
        f_hi = face[k, 1] * v
        edge[...] = f_hi.reshape(flat)
        xhi_out[rnd] = edge[pl.ds(nx - 1, comps * nch, stride=nx), :]

        @pl.when(has_xhi)
        def _():
            neighbour_copy(
                xhi_out.at[rnd], xlo_in.at[rnd], send_sem.at[0], xlo_sem.at[rnd], (mx + 1, my)
            ).start()

        f_lo = face[k, 0] * v
        edge[...] = f_lo.reshape(flat)
        xlo_out[rnd] = edge[pl.ds(0, comps * nch, stride=nx), :]

        @pl.when(has_xlo)
        def _():
            neighbour_copy(
                xlo_out.at[rnd], xhi_in.at[rnd], send_sem.at[1], xhi_sem.at[rnd], (mx - 1, my)
            ).start()

        g = pltpu.roll((face[k, 3] * v).reshape(flat), 1, axis=1).reshape(cells)
        wrap = jnp.concatenate([g[:, rows - nx :], g[:, : rows - nx]], axis=1)
        is_lane = lane_ids == 0
        is_rim = jnp.logical_and(is_lane, row_ids < nx)
        yhi_out[rnd] = jnp.where(is_lane[:, :nx], wrap[:, :nx], 0.0).reshape(comps * nx, LANES)

        @pl.when(has_yhi)
        def _():
            neighbour_copy(
                yhi_out.at[rnd], ylo_in.at[rnd], send_sem.at[2], ylo_sem.at[rnd], (mx, my + 1)
            ).start()

        from_ylo = jnp.where(is_rim, 0.0, jnp.where(is_lane, wrap, g))
        g = pltpu.roll((face[k, 2] * v).reshape(flat), LANES - 1, axis=1).reshape(cells)
        wrap = jnp.concatenate([g[:, nx:], g[:, :nx]], axis=1)
        is_lane = lane_ids == LANES - 1
        is_rim = jnp.logical_and(is_lane, row_ids >= rows - nx)
        ylo_out[rnd] = jnp.where(is_lane[:, rows - nx :], wrap[:, rows - nx :], 0.0).reshape(
            comps * nx, LANES
        )

        @pl.when(has_ylo)
        def _():
            neighbour_copy(
                ylo_out.at[rnd], yhi_in.at[rnd], send_sem.at[3], yhi_sem.at[rnd], (mx, my - 1)
            ).start()

        from_yhi = jnp.where(is_rim, 0.0, jnp.where(is_lane, wrap, g))

        picked = exact_dot(v.reshape(flat), lane_sel)
        weighted = jnp.sum(row_w * picked, axis=0, keepdims=True)
        well_part = exact_dot(jnp.broadcast_to(weighted, (8, nperf)), well_sel, transposed=True)
        message = jnp.where(sub_ids == 0, well_part, 0.0)
        message = add_dots(message, dots)
        start_gy(rnd, message)

        total = diag[k, 0] * v[0][None]
        for j in range(1, comps):
            total = total + diag[k, j] * v[j][None]
        down = jnp.concatenate([f_hi[:, rows - 1 :], f_hi[:, : rows - 1]], axis=1)
        up = jnp.concatenate([f_lo[:, 1:], f_lo[:, :1]], axis=1)
        total = total - from_ylo - from_yhi
        total = total - jnp.where(x_ids == 0, 0.0, down)
        total = total - jnp.where(x_ids == nx - 1, 0.0, up)
        acc[...] = total.reshape(flat)

        summed = end_gy(rnd)
        if dots is not None:
            start_gx(rnd, summed)
        per_well = jnp.where(sub_ids == 0, summed * inv_well, 0.0)
        per_perf = jnp.sum(exact_dot(per_well, well_sel), axis=0, keepdims=True)
        moved = exact_dot(col_w * per_perf, lane_sel, transposed=True)

        @pl.when(has_xlo)
        def _():
            wait_bytes(xlo_in.at[rnd], xlo_sem.at[rnd])

        @pl.when(has_xhi)
        def _():
            wait_bytes(xhi_in.at[rnd], xhi_sem.at[rnd])

        @pl.when(has_ylo)
        def _():
            wait_bytes(ylo_in.at[rnd], ylo_sem.at[rnd])

        @pl.when(has_yhi)
        def _():
            wait_bytes(yhi_in.at[rnd], yhi_sem.at[rnd])

        acc[...] = acc[...] - moved
        lo_rows = pl.ds(0, comps * nch, stride=nx)
        hi_rows = pl.ds(nx - 1, comps * nch, stride=nx)
        acc[lo_rows, :] = acc[lo_rows, :] - xlo_in[rnd]
        acc[hi_rows, :] = acc[hi_rows, :] - xhi_in[rnd]
        for c in range(comps):
            first = pl.ds(c * rows, nx)
            last = pl.ds(c * rows + rows - nx, nx)
            part = pl.ds(c * nx, nx)
            acc[first, :] = acc[first, :] - ylo_in[rnd, part, :]
            acc[last, :] = acc[last, :] - yhi_in[rnd, part, :]
        return acc[...].reshape(cells)

    def add_dots(message, dots):
        if dots is None:
            return message
        a, b = dots
        a = jnp.sum(a.reshape(flat), axis=0, keepdims=True)
        b = jnp.sum(b.reshape(flat), axis=0, keepdims=True)
        return jnp.where(sub_ids == 1, a, jnp.where(sub_ids == 2, b, message))

    def start_gy(rnd, message):
        gy_buf[rnd, my] = message
        for d in range(1, ngy):
            neighbour_copy(
                gy_buf.at[rnd, my],
                gy_buf.at[rnd, my],
                send_sem.at[4],
                gy_sem.at[rnd],
                (mx, lax.rem(my + d, ngy)),
            ).start()

    def end_gy(rnd):
        wait_bytes(gy_buf.at[rnd, pl.ds(0, ngy - 1)], gy_sem.at[rnd])
        return jnp.sum(gy_buf[rnd], axis=0)

    def start_gx(rnd, message):
        gx_buf[rnd, mx] = message
        for d in range(1, ngx):
            neighbour_copy(
                gx_buf.at[rnd, mx],
                gx_buf.at[rnd, mx],
                send_sem.at[5],
                gx_sem.at[rnd],
                (lax.rem(mx + d, ngx), my),
            ).start()

    def end_gx(rnd):
        wait_bytes(gx_buf.at[rnd, pl.ds(0, ngx - 1)], gx_sem.at[rnd])
        totals = jnp.sum(jnp.sum(gx_buf[rnd], axis=0), axis=1, keepdims=True)
        return totals[1:2] / totals[2:3]

    inv_well = jnp.float32(1.0) / wdiag_ref[...]

    loads[3].wait()
    loads[4].wait()
    loads[5].wait()
    loads[6].wait()

    pl.semaphore_wait(barrier, ngx + ngy - 2)

    adjoint = None
    rnd = 0
    for k in range(steps - 1, -1, -1):
        row_w = spread(pcoef_ref[k, 0])
        col_w = spread(pcoef_ref[k, 1])
        residual = weight[...] * states[k]
        if adjoint is not None:
            residual = residual + accum[...] * adjoint
        search = apply_precond(residual)
        image = operator(k, rnd, search, row_w, col_w, None)
        rnd += 1
        solution = None
        for sweep in range(SWEEPS):
            dots = (residual * image, image * image)
            if sweep < SWEEPS - 1:
                pre_image = apply_precond(image)
                next_image = operator(k, rnd, pre_image, row_w, col_w, dots)
            else:
                start_gy(rnd, add_dots(jnp.zeros((8, LANES), jnp.float32), dots))
                start_gx(rnd, end_gy(rnd))
            step_len = end_gx(rnd)
            rnd += 1
            moved = step_len * search.reshape(flat)
            solution = moved if solution is None else solution + moved
            if sweep < SWEEPS - 1:
                residual = residual - (step_len * image.reshape(flat)).reshape(cells)
                search = search - (step_len * pre_image.reshape(flat)).reshape(cells)
                image = image - (step_len * next_image.reshape(flat)).reshape(cells)
        adjoint = solution.reshape(cells)
        out_ref[k] = adjoint

    ops = steps * SWEEPS

    @pl.when(has_xhi)
    def _():
        wait_bytes(xhi_out.at[pl.ds(0, ops)], send_sem.at[0])

    @pl.when(has_xlo)
    def _():
        wait_bytes(xlo_out.at[pl.ds(0, ops)], send_sem.at[1])

    @pl.when(has_yhi)
    def _():
        wait_bytes(yhi_out.at[pl.ds(0, ops)], send_sem.at[2])

    @pl.when(has_ylo)
    def _():
        wait_bytes(ylo_out.at[pl.ds(0, ops)], send_sem.at[3])

    wait_bytes(gy_buf.at[:, pl.ds(0, ngy - 1)], send_sem.at[4])
    wait_bytes(gx_buf.at[pl.ds(0, ops), pl.ds(0, ngx - 1)], send_sem.at[5])


def to_rows(x):
    lead = x.shape[:-2]
    nx, ny = x.shape[-2:]
    x = x.reshape(*lead, nx, ny // LANES, LANES)
    return jnp.swapaxes(x, -3, -2).reshape(*lead, nx * (ny // LANES), LANES)


def local(
    ngx,
    ngy,
    base_state,
    misfit_weight,
    state_deltas,
    delta_index,
    diag_block,
    precond,
    face_coupling,
    accumulation,
    well_diag,
    perf_well,
    perf_cell,
    perf_coef,
):
    comps, nx, ny = base_state.shape
    nch = ny // LANES
    rows = nx * nch
    steps = diag_block.shape[0]
    nwells = well_diag.shape[0]
    nperf = perf_cell.shape[-1]
    rounds = steps * (SWEEPS + 1)
    f32 = jnp.float32
    big = [to_rows(a) for a in (base_state, misfit_weight, state_deltas)]
    big2 = [to_rows(a) for a in (diag_block, precond, face_coupling, accumulation)]
    wdiag = jnp.pad(well_diag, (0, LANES - nwells), constant_values=1.0).reshape(1, LANES)
    any_spec = pl.BlockSpec(memory_space=pl.ANY)
    vmem = pl.BlockSpec(memory_space=pltpu.VMEM)
    smem = pl.BlockSpec(memory_space=pltpu.SMEM)
    xh = pltpu.VMEM((rounds, comps * nch, LANES), f32)
    yh = pltpu.VMEM((rounds, comps * nx, LANES), f32)
    result = pl.pallas_call(
        functools.partial(kernel, ngx, ngy, comps, nx, nch, nwells, steps),
        out_shape=jax.ShapeDtypeStruct((steps, comps, rows, LANES), f32),
        in_specs=[any_spec] * 3 + [smem] + [any_spec] * 4 + [vmem] * 4,
        out_specs=vmem,
        scratch_shapes=[
            pltpu.VMEM(big[0].shape, f32),
            pltpu.VMEM(big[1].shape, f32),
            pltpu.VMEM(big[2].shape, big[2].dtype),
            pltpu.VMEM(big2[0].shape, f32),
            pltpu.VMEM(big2[1].shape, f32),
            pltpu.VMEM(big2[2].shape, f32),
            pltpu.VMEM(big2[3].shape, f32),
            pltpu.VMEM((comps * rows, LANES), f32),
            pltpu.VMEM((comps * rows, LANES), f32),
            xh,
            xh,
            yh,
            yh,
            xh,
            xh,
            yh,
            yh,
            pltpu.VMEM((rounds, ngy, 8, LANES), f32),
            pltpu.VMEM((rounds, ngx, 8, LANES), f32),
            pltpu.SemaphoreType.DMA((7,)),
            pltpu.SemaphoreType.DMA((6,)),
            pltpu.SemaphoreType.DMA((rounds,)),
            pltpu.SemaphoreType.DMA((rounds,)),
            pltpu.SemaphoreType.DMA((rounds,)),
            pltpu.SemaphoreType.DMA((rounds,)),
            pltpu.SemaphoreType.DMA((rounds,)),
            pltpu.SemaphoreType.DMA((rounds,)),
        ],
        compiler_params=pltpu.CompilerParams(
            collective_id=0, has_side_effects=True, vmem_limit_bytes=32 * 1024 * 1024
        ),
    )(
        big[0],
        big[1],
        big[2],
        delta_index,
        big2[0],
        big2[1],
        big2[2],
        big2[3],
        wdiag,
        perf_well.reshape(1, 1, nperf),
        perf_cell.reshape(1, 1, nperf),
        perf_coef.reshape(steps, 2, comps, nperf),
    )
    result = result.reshape(steps, comps, nch, nx, LANES)
    return jnp.swapaxes(result, -3, -2).reshape(steps, comps, nx, ny)


def solution(mesh):
    ngx, ngy = mesh.shape["gx"], mesh.shape["gy"]
    return jax.shard_map(
        functools.partial(local, ngx, ngy),
        mesh=mesh,
        in_specs=(
            P(None, "gx", "gy"),
            P(None, "gx", "gy"),
            P(None, None, "gx", "gy"),
            P(),
            P(None, None, None, "gx", "gy"),
            P(None, None, "gx", "gy"),
            P(None, None, None, "gx", "gy"),
            P(None, "gx", "gy"),
            P("gx"),
            P("gx", "gy", None),
            P("gx", "gy", None),
            P(None, None, None, "gx", "gy", None),
        ),
        out_specs=P(None, None, "gx", "gy"),
        check_vma=False,
    )
```

time: 619 us -> 82.1 us (0.13)
  blocking collectives: 425 us -> 0 us
  starting transfers between devices: 105 us -> 0 us
  Pallas kernels: 0 us -> 72.1 us
  other arithmetic: 41 us -> 0 us
  local copies, waits for them, and re-layouts: 25.4 us -> 9.46 us
  between operations: 11.6 us -> 0.02 us
    psum x16 -> x0, blocking collectives: 425 us -> none  [the longest x8 342 us: local(): lax.psum((jnp.sum(residual * image), jnp.sum(image * image)), ('gx', 'gy'))]
    ppermute x40 -> x0, starting transfers between devices: 105 us -> none  [the longest x20 78.4 us: with_halo(): lax.ppermute(tail, axis, [(i, (i + 1) % count) for i in range(ends)])]
    pallas_call x0 -> x1, Pallas kernels: none -> 72.1 us  [local(): pl.pallas_call(functools.partial(kernel, ngx, ngy, comps, nx, nch, nwells...]
    reduce_sum x17 -> x0, other arithmetic: 17.2 us -> none  [the longest x8 14.2 us: local(): jnp.sum(image * image)]
    scatter-add x8 -> x0, other arithmetic: 11.6 us -> none  [local(): flattened = flattened.at[:, cell_ids].add(col_coef * per_perf[None, :])]
  transfers between devices with their start and end apart: 40 -> 0, of which waited for: 7 -> 0; matrix products, arithmetic and copies ran while one was open for 8% -> 0% of each run, Pallas kernels for 0% -> 0%
where the time goes in v1:
time: 82.1 us; the launch traced here: 81.6 us
  Pallas kernels  72.1 us (88%)
  local copies, waits for them, and re-layouts  9.46 us (12%)
    pallas_call x1, Pallas kernels, local(): pl.pallas_call(functools.partial(kernel, ngx, ngy, comps, nx, nch, nwells...  72.1 us
    unnamed x23, local copies, waits for them, and re-layouts  8.77 us

profile of v1, /device:TPU:0, one launch (start us, length us, event | category | flops | bytes accessed | tf_op | source)
XLA Modules:
  0.0 81.6 jit_solution(5219658617266407546)
XLA Ops:
  0.0 0.0 copy-start.7
  0.0 0.0 copy-start.8
  0.0 0.7 pad_bitcast_fusion.wdiag_ref
  0.7 0.0 copy-done.7
  0.7 0.0 copy-done.8
  0.7 0.0 copy-start
  0.7 1.2 %copy-done = f32[2,8,8,4,512]{4,3,2,1,0:T(4,128)S(1)} copy-done((f32[2,8,8,4,512]{4,3,2,1,0:T(4,128)S(1)}, f32[2,8,8,4,512]{4,3,2,1,0:T(4,128)}, u32[]{:S(2)}) %copy-start) | copy-done | bytes 1048600
  1.9 0.0 copy-start.1
  1.9 1.0 %copy-done.1 = f32[8,8,4,512]{3,2,1,0:T(4,128)S(1)} copy-done((f32[8,8,4,512]{3,2,1,0:T(4,128)S(1)}, f32[8,8,4,512]{3,2,1,0:T(4,128)}, u32[]{:S(2)}) %copy-start.1) | copy-done | bytes 524312
  3.0 0.0 copy-start.2
  3.0 1.0 %copy-done.2 = f32[2,4,8,4,512]{4,3,2,1,0:T(4,128)S(1)} copy-done((f32[2,4,8,4,512]{4,3,2,1,0:T(4,128)S(1)}, f32[2,4,8,4,512]{4,3,2,1,0:T(4,128)}, u32[]{:S(2)}) %copy-start.2) | copy-done | bytes 524312
  4.0 0.0 copy-start.3
  4.0 0.9 %copy-done.3 = bf16[8,8,4,512]{3,2,1,0:T(4,128)(2,1)S(1)} copy-done((bf16[8,8,4,512]{3,2,1,0:T(4,128)(2,1)S(1)}, bf16[8,8,4,512]{3,2,1,0:T(4,128)(2,1)}, u32[]{:S(2)}) %copy-start.3) | copy-done | bytes 262168
  5.0 0.0 copy-start.4
  5.0 0.8 %copy-done.4 = f32[8,4,512]{2,1,0:T(4,128)S(1)} copy-done((f32[8,4,512]{2,1,0:T(4,128)S(1)}, f32[8,4,512]{2,1,0:T(4,128)}, u32[]{:S(2)}) %copy-start.4) | copy-done | bytes 65560
  5.8 0.0 copy-start.5
  5.8 0.8 %copy-done.5 = f32[8,4,512]{2,1,0:T(4,128)S(1)} copy-done((f32[8,4,512]{2,1,0:T(4,128)S(1)}, f32[8,4,512]{2,1,0:T(4,128)}, u32[]{:S(2)}) %copy-start.5) | copy-done | bytes 65560
  6.7 0.0 copy-start.6
  6.7 0.8 %copy-done.6 = f32[8,4,512]{2,1,0:T(4,128)S(1)} copy-done((f32[8,4,512]{2,1,0:T(4,128)S(1)}, f32[8,4,512]{2,1,0:T(4,128)}, u32[]{:S(2)}) %copy-start.6) | copy-done | bytes 65560
  7.5 0.0 copy-start.9
  7.5 0.7 copy-done.9
  8.2 0.0 copy-start.10
  8.2 0.7 copy-done.10
  8.8 72.1 %shard_map.118 = f32[2,8,16,128]{3,2,1,0:T(8,128)S(1)} custom-call(f32[8,16,128]{2,1,0:T(8,128)S(1)} %bitcast.48, f32[8,16,128]{2,1,0:T(8,128)S(1)} %bitcast.49, bf16[8,8,16,128]{3,2,1,0:T(8,128)(2,1)S(1)} %bitcast.47, s32[2,8]{1,0:T(2,128)S(1)} %copy-done.8, f32[2,8,8,16,128]{4,3,2,1,0:T(8,128)S(1)} %bitcast.43, f32[8,8,16,128]{3,2,1,0:T(8,128)S(1)} %bitcast.44, ...), custom_call_target="tpu_custom_call" | custom-call | tf_op jit(solution)/shard_map/pallas_call | solution.py:425
  81.0 0.7 copy.22
Async XLA Ops:
  0.0 0.7 copy-start.7
  0.0 0.7 copy-start.8
  0.7 1.2 %copy-start = (f32[2,8,8,4,512]{4,3,2,1,0:T(4,128)S(1)}, f32[2,8,8,4,512]{4,3,2,1,0:T(4,128)}, u32[]{:S(2)}) copy-start(f32[2,8,8,4,512]{4,3,2,1,0:T(4,128)} %param.16) | copy-start | bytes 3145732
  1.9 1.0 %copy-start.1 = (f32[8,8,4,512]{3,2,1,0:T(4,128)S(1)}, f32[8,8,4,512]{3,2,1,0:T(4,128)}, u32[]{:S(2)}) copy-start(f32[8,8,4,512]{3,2,1,0:T(4,128)} %param.17) | copy-start | bytes 1572868
  3.0 1.0 %copy-start.2 = (f32[2,4,8,4,512]{4,3,2,1,0:T(4,128)S(1)}, f32[2,4,8,4,512]{4,3,2,1,0:T(4,128)}, u32[]{:S(2)}) copy-start(f32[2,4,8,4,512]{4,3,2,1,0:T(4,128)} %param.18) | copy-start | bytes 1572868
  4.0 0.9 %copy-start.3 = (bf16[8,8,4,512]{3,2,1,0:T(4,128)(2,1)S(1)}, bf16[8,8,4,512]{3,2,1,0:T(4,128)(2,1)}, u32[]{:S(2)}) copy-start(bf16[8,8,4,512]{3,2,1,0:T(4,128)(2,1)} %param.14) | copy-start | bytes 786436
  5.0 0.8 %copy-start.4 = (f32[8,4,512]{2,1,0:T(4,128)S(1)}, f32[8,4,512]{2,1,0:T(4,128)}, u32[]{:S(2)}) copy-start(f32[8,4,512]{2,1,0:T(4,128)} %param.12) | copy-start | bytes 196612
  5.8 0.8 %copy-start.5 = (f32[8,4,512]{2,1,0:T(4,128)S(1)}, f32[8,4,512]{2,1,0:T(4,128)}, u32[]{:S(2)}) copy-start(f32[8,4,512]{2,1,0:T(4,128)} %param.13) | copy-start | bytes 196612
  6.7 0.8 %copy-start.6 = (f32[8,4,512]{2,1,0:T(4,128)S(1)}, f32[8,4,512]{2,1,0:T(4,128)}, u32[]{:S(2)}) copy-start(f32[8,4,512]{2,1,0:T(4,128)} %param.19) | copy-start | bytes 196612
  7.5 0.7 copy-start.9
  8.2 0.7 copy-start.10

commit v2 on v1

v2 whole, which is shorter than its diff:
```python
import functools

import jax
import jax.numpy as jnp
from jax import lax
from jax.experimental import pallas as pl
from jax.experimental.pallas import tpu as pltpu
from jax.sharding import PartitionSpec as P

BATCH = 3
LANES = 128
MESH = pl.DeviceIdType.MESH


def split3(x):
    a = x.astype(jnp.bfloat16)
    rest = x - a.astype(jnp.float32)
    b = rest.astype(jnp.bfloat16)
    c = (rest - b.astype(jnp.float32)).astype(jnp.bfloat16)
    return jnp.concatenate([a, b, c], axis=0)


def exact_dot(x, sel, transposed=False):
    rows = x.shape[0]
    dims = (((1,), (1 if transposed else 0,)), ((), ()))
    out = lax.dot_general(split3(x), sel, dims, preferred_element_type=jnp.float32)
    return out[:rows] + out[rows : 2 * rows] + out[2 * rows :]


def kernel(
    ngx,
    ngy,
    comps,
    nx,
    nch,
    nwells,
    steps,
    base_hbm,
    weight_hbm,
    deltas_hbm,
    index_hbm,
    diag_hbm,
    precond_hbm,
    face_hbm,
    accum_hbm,
    wdiag_hbm,
    pwell_hbm,
    pcell_hbm,
    pcoef_hbm,
    out_ref,
    base,
    weight,
    deltas,
    diag,
    precond,
    face,
    accum,
    index_ref,
    wdiag_ref,
    pwell_ref,
    pcell_ref,
    pcoef_ref,
    acc,
    edge,
    xlo_out,
    xhi_out,
    ylo_out,
    yhi_out,
    xlo_in,
    xhi_in,
    ylo_in,
    yhi_in,
    gy_buf,
    gx_buf,
    load_sem,
    send_sem,
    xlo_sem,
    xhi_sem,
    ylo_sem,
    yhi_sem,
    gy_sem,
    gx_sem,
):
    rows = nx * nch
    cells = (comps, rows, LANES)
    flat = (comps * rows, LANES)
    mx = lax.axis_index("gx")
    my = lax.axis_index("gy")
    has_xlo, has_xhi = mx > 0, mx < ngx - 1
    has_ylo, has_yhi = my > 0, my < ngy - 1

    loads = []
    order = (
        (pcell_hbm, pcell_ref),
        (pwell_hbm, pwell_ref),
        (index_hbm, index_ref),
        (wdiag_hbm, wdiag_ref),
        (pcoef_hbm, pcoef_ref),
        (base_hbm, base),
        (weight_hbm, weight),
        (deltas_hbm, deltas),
        (precond_hbm, precond),
        (face_hbm, face),
        (diag_hbm, diag),
        (accum_hbm, accum),
    )
    for n, (src, dst) in enumerate(order):
        cp = pltpu.make_async_copy(src, dst, load_sem.at[n])
        cp.start()
        loads.append(cp)

    barrier = pltpu.get_barrier_semaphore()
    for d in range(1, ngx):
        pl.semaphore_signal(
            barrier, inc=1, device_id=(lax.rem(mx + d, ngx), my), device_id_type=MESH
        )
    for d in range(1, ngy):
        pl.semaphore_signal(
            barrier, inc=1, device_id=(mx, lax.rem(my + d, ngy)), device_id_type=MESH
        )

    @pl.when(jnp.logical_not(has_xlo))
    def _():
        xlo_in[...] = jnp.zeros_like(xlo_in)

    @pl.when(jnp.logical_not(has_xhi))
    def _():
        xhi_in[...] = jnp.zeros_like(xhi_in)

    @pl.when(jnp.logical_not(has_ylo))
    def _():
        ylo_in[...] = jnp.zeros_like(ylo_in)

    @pl.when(jnp.logical_not(has_yhi))
    def _():
        yhi_in[...] = jnp.zeros_like(yhi_in)

    loads[0].wait()
    loads[1].wait()
    pcell = pcell_ref[0]
    length_y = nch * LANES
    p_lane = lax.rem(pcell, LANES)
    p_row = lax.rem(lax.div(pcell, LANES), nch) * nx + lax.div(pcell, length_y)
    nperf = pcell.shape[-1]
    lane_sel = (
        (lax.broadcasted_iota(jnp.int32, (LANES, nperf), 0) == p_lane)
        .astype(jnp.float32)
        .astype(jnp.bfloat16)
    )
    row_mask = lax.broadcasted_iota(jnp.int32, (rows, nperf), 0) == p_row
    well_mask = lax.broadcasted_iota(jnp.int32, (LANES, nperf), 0) == pwell_ref[0]
    well_sel = well_mask.astype(jnp.float32).astype(jnp.bfloat16)
    lane_ids = lax.broadcasted_iota(jnp.int32, (1, rows, LANES), 2)
    row_ids = lax.broadcasted_iota(jnp.int32, (1, rows, LANES), 1)
    sub_ids = lax.broadcasted_iota(jnp.int32, (8, LANES), 0)
    x_ids = lax.rem(row_ids, nx)

    for n in (2, 3, 4, 5, 6, 7):
        loads[n].wait()
    states = []
    running = base[...]
    for k in range(steps):
        picked = [
            deltas[index_ref[k, c], c].astype(jnp.float32)[None] for c in range(comps)
        ]
        running = running + jnp.concatenate(picked, axis=0)
        states.append(running)

    def spread(c_row):
        full = jnp.where(row_mask[None], c_row[:, None, :], jnp.float32(0.0))
        return full.reshape(comps * rows, nperf)

    def apply_precond(v):
        total = precond[:, 0] * v[0][None]
        for j in range(1, comps):
            total = total + precond[:, j] * v[j][None]
        return total

    def neighbour_copy(src, dst, sem_out, sem_in, target):
        return pltpu.make_async_remote_copy(
            src_ref=src,
            dst_ref=dst,
            send_sem=sem_out,
            recv_sem=sem_in,
            device_id=target,
            device_id_type=MESH,
        )

    def wait_bytes(ref, sem):
        pltpu.make_async_copy(ref, ref, sem).wait()

    def operator(k, rnd, slots, vs, row_w, col_w, grams, gx_rnd):
        picked = exact_dot(jnp.concatenate([v.reshape(flat) for v in vs], axis=0), lane_sel)
        weighted = jnp.zeros((8, nperf), jnp.float32)
        for n in range(len(vs)):
            part = picked[n * comps * rows : (n + 1) * comps * rows]
            part = jnp.sum(row_w * part, axis=0, keepdims=True)
            weighted = jnp.where(sub_ids == n, part, weighted)
        start_gy(rnd, add_grams(exact_dot(weighted, well_sel, transposed=True), grams))
        kept = []
        for slot, v in zip(slots, vs):
            kept.append(send_halos(k, slot, v))

        for n, v in enumerate(vs):
            f_hi, f_lo, from_y = kept[n]
            total = diag[k, 0] * v[0][None]
            for j in range(1, comps):
                total = total + diag[k, j] * v[j][None]
            down = jnp.concatenate([f_hi[:, rows - 1 :], f_hi[:, : rows - 1]], axis=1)
            up = jnp.concatenate([f_lo[:, 1:], f_lo[:, :1]], axis=1)
            total = total - from_y
            total = total - jnp.where(x_ids == 0, 0.0, down)
            total = total - jnp.where(x_ids == nx - 1, 0.0, up)
            acc[n] = total.reshape(flat)

        for slot in slots:

            @pl.when(has_xlo)
            def _(slot=slot):
                wait_bytes(xlo_in.at[slot], xlo_sem.at[slot])

            @pl.when(has_xhi)
            def _(slot=slot):
                wait_bytes(xhi_in.at[slot], xhi_sem.at[slot])

            @pl.when(has_ylo)
            def _(slot=slot):
                wait_bytes(ylo_in.at[slot], ylo_sem.at[slot])

            @pl.when(has_yhi)
            def _(slot=slot):
                wait_bytes(yhi_in.at[slot], yhi_sem.at[slot])

        for n, slot in enumerate(slots):
            mine = acc.at[n]
            lo_rows = pl.ds(0, comps * nch, stride=nx)
            hi_rows = pl.ds(nx - 1, comps * nch, stride=nx)
            mine[lo_rows, :] = mine[lo_rows, :] - xlo_in[slot]
            mine[hi_rows, :] = mine[hi_rows, :] - xhi_in[slot]
            for c in range(comps):
                first = pl.ds(c * rows, nx)
                last = pl.ds(c * rows + rows - nx, nx)
                part = pl.ds(c * nx, nx)
                mine[first, :] = mine[first, :] - ylo_in[slot, part, :]
                mine[last, :] = mine[last, :] - yhi_in[slot, part, :]

        summed = end_gy(rnd)
        if grams is not None:
            start_gx(gx_rnd, summed)
        per_perf = exact_dot(summed * inv_well, well_sel)
        moved = [col_w * per_perf[n : n + 1] for n in range(len(vs))]
        moved = exact_dot(jnp.concatenate(moved, axis=0), lane_sel, transposed=True)
        size = comps * rows
        return [
            (acc[n] - moved[n * size : (n + 1) * size]).reshape(cells) for n in range(len(vs))
        ]

    def send_halos(k, slot, v):
        f_hi = face[k, 1] * v
        edge[0] = f_hi.reshape(flat)
        xhi_out[slot] = edge[0, pl.ds(nx - 1, comps * nch, stride=nx), :]

        @pl.when(has_xhi)
        def _():
            neighbour_copy(
                xhi_out.at[slot], xlo_in.at[slot], send_sem.at[0], xlo_sem.at[slot], (mx + 1, my)
            ).start()

        f_lo = face[k, 0] * v
        edge[1] = f_lo.reshape(flat)
        xlo_out[slot] = edge[1, pl.ds(0, comps * nch, stride=nx), :]

        @pl.when(has_xlo)
        def _():
            neighbour_copy(
                xlo_out.at[slot], xhi_in.at[slot], send_sem.at[1], xhi_sem.at[slot], (mx - 1, my)
            ).start()

        g = pltpu.roll((face[k, 3] * v).reshape(flat), 1, axis=1).reshape(cells)
        wrap = jnp.concatenate([g[:, rows - nx :], g[:, : rows - nx]], axis=1)
        is_lane = lane_ids == 0
        is_rim = jnp.logical_and(is_lane, row_ids < nx)
        yhi_out[slot] = jnp.where(is_lane[:, :nx], wrap[:, :nx], 0.0).reshape(comps * nx, LANES)

        @pl.when(has_yhi)
        def _():
            neighbour_copy(
                yhi_out.at[slot], ylo_in.at[slot], send_sem.at[2], ylo_sem.at[slot], (mx, my + 1)
            ).start()

        from_ylo = jnp.where(is_rim, 0.0, jnp.where(is_lane, wrap, g))
        g = pltpu.roll((face[k, 2] * v).reshape(flat), LANES - 1, axis=1).reshape(cells)
        wrap = jnp.concatenate([g[:, nx:], g[:, :nx]], axis=1)
        is_lane = lane_ids == LANES - 1
        is_rim = jnp.logical_and(is_lane, row_ids >= rows - nx)
        ylo_out[slot] = jnp.where(is_lane[:, rows - nx :], wrap[:, rows - nx :], 0.0).reshape(
            comps * nx, LANES
        )

        @pl.when(has_ylo)
        def _():
            neighbour_copy(
                ylo_out.at[slot], yhi_in.at[slot], send_sem.at[3], yhi_sem.at[slot], (mx, my - 1)
            ).start()

        return f_hi, f_lo, from_ylo + jnp.where(is_rim, 0.0, jnp.where(is_lane, wrap, g))

    def grams_of(q0, q1, q2):
        return (q0 * q1, q1 * q1, q0 * q2, q1 * q2, q2 * q2)

    def add_grams(message, grams):
        if grams is None:
            return message
        for n, g in enumerate(grams):
            total = jnp.sum(g.reshape(flat), axis=0, keepdims=True)
            message = jnp.where(sub_ids == BATCH + n, total, message)
        return message

    def start_gy(rnd, message):
        gy_buf[rnd, my] = message
        for d in range(1, ngy):
            neighbour_copy(
                gy_buf.at[rnd, my],
                gy_buf.at[rnd, my],
                send_sem.at[4],
                gy_sem.at[rnd],
                (mx, lax.rem(my + d, ngy)),
            ).start()

    def end_gy(rnd):
        wait_bytes(gy_buf.at[rnd, pl.ds(0, ngy - 1)], gy_sem.at[rnd])
        return jnp.sum(gy_buf[rnd], axis=0)

    def start_gx(rnd, message):
        gx_buf[rnd, mx] = message
        for d in range(1, ngx):
            neighbour_copy(
                gx_buf.at[rnd, mx],
                gx_buf.at[rnd, mx],
                send_sem.at[5],
                gx_sem.at[rnd],
                (lax.rem(mx + d, ngx), my),
            ).start()

    def end_gx(rnd):
        wait_bytes(gx_buf.at[rnd, pl.ds(0, ngx - 1)], gx_sem.at[rnd])
        totals = jnp.sum(jnp.sum(gx_buf[rnd], axis=0), axis=1, keepdims=True)
        g01, g11, g02, g12, g22 = (totals[BATCH + n : BATCH + n + 1] for n in range(5))
        first = g01 / g11
        second = (
            first * (first * g12 - g02) / (g11 - 2.0 * first * g12 + first * first * g22)
        )
        return (first + second)[None], (first * second)[None]

    inv_well = jnp.concatenate(
        [jnp.float32(1.0) / wdiag_ref[...], jnp.ones((1, LANES - nwells), jnp.float32)], axis=1
    )

    for n in (8, 9, 10, 11):
        loads[n].wait()

    pl.semaphore_wait(barrier, ngx + ngy - 2)

    gy_rnd = gx_rnd = slot = 0
    late = None
    for k in range(steps - 1, -1, -1):
        row_w = spread(pcoef_ref[k, 0])
        col_w = spread(pcoef_ref[k, 1])
        v0 = weight[...] * states[k]
        if late is None:
            u0 = apply_precond(v0)
            (v1,) = operator(k, gy_rnd, [slot], [u0], row_w, col_w, None, None)
            slot += 1
        else:
            grams, part, p0, p1 = late
            starts = [v0 + accum[...] * part, accum[...] * p0, accum[...] * p1]
            firsts = [apply_precond(v) for v in starts]
            slots = [slot + n for n in range(BATCH)]
            images = operator(k, gy_rnd, slots, firsts, row_w, col_w, grams, gx_rnd)
            slot += BATCH
            both, prod = end_gx(gx_rnd)
            gx_rnd += 1
            out_ref[k + 1] = part + both * p0 - prod * p1
            v0, u0, v1 = (a + both * b - prod * c for a, b, c in (starts, firsts, images))
        gy_rnd += 1
        u1 = apply_precond(v1)
        (v2,) = operator(k, gy_rnd, [slot], [u1], row_w, col_w, None, None)
        u2 = apply_precond(v2)
        grams = grams_of(v0, v1, v2)
        (v3,) = operator(k, gy_rnd + 1, [slot + 1], [u2], row_w, col_w, grams, gx_rnd)
        u3 = apply_precond(v3)
        (v4,) = operator(k, gy_rnd + 2, [slot + 2], [u3], row_w, col_w, None, None)
        gy_rnd += 3
        slot += 3
        both, prod = end_gx(gx_rnd)
        gx_rnd += 1
        q0 = v0 - both * v1 + prod * v2
        q1 = v1 - both * v2 + prod * v3
        q2 = v2 - both * v3 + prod * v4
        part = both * u0 - prod * u1
        p0 = u0 - both * u1 + prod * u2
        p1 = u1 - both * u2 + prod * u3
        late = grams_of(q0, q1, q2), part, p0, p1
    grams, part, p0, p1 = late
    start_gy(gy_rnd, add_grams(jnp.zeros((8, LANES), jnp.float32), grams))
    start_gx(gx_rnd, end_gy(gy_rnd))
    both, prod = end_gx(gx_rnd)
    out_ref[0] = part + both * p0 - prod * p1

    @pl.when(has_xhi)
    def _():
        wait_bytes(xhi_out, send_sem.at[0])

    @pl.when(has_xlo)
    def _():
        wait_bytes(xlo_out, send_sem.at[1])

    @pl.when(has_yhi)
    def _():
        wait_bytes(yhi_out, send_sem.at[2])

    @pl.when(has_ylo)
    def _():
        wait_bytes(ylo_out, send_sem.at[3])

    wait_bytes(gy_buf.at[:, pl.ds(0, ngy - 1)], send_sem.at[4])
    wait_bytes(gx_buf.at[:, pl.ds(0, ngx - 1)], send_sem.at[5])


def to_rows(x):
    lead = x.shape[:-2]
    nx, ny = x.shape[-2:]
    x = x.reshape(*lead, nx, ny // LANES, LANES)
    return jnp.swapaxes(x, -3, -2).reshape(*lead, nx * (ny // LANES), LANES)


def local(
    ngx,
    ngy,
    base_state,
    misfit_weight,
    state_deltas,
    delta_index,
    diag_block,
    precond,
    face_coupling,
    accumulation,
    well_diag,
    perf_well,
    perf_cell,
    perf_coef,
):
    comps, nx, ny = base_state.shape
    nch = ny // LANES
    rows = nx * nch
    steps = diag_block.shape[0]
    nwells = well_diag.shape[0]
    nperf = perf_cell.shape[-1]
    slots = 4 + (steps - 1) * (BATCH + 3)
    gy_rounds = 4 * steps + 1
    gx_rounds = 2 * steps
    f32 = jnp.float32
    big = [to_rows(a) for a in (base_state, misfit_weight, state_deltas)]
    big2 = [to_rows(a) for a in (diag_block, precond, face_coupling, accumulation)]
    any_spec = pl.BlockSpec(memory_space=pl.ANY)
    vmem = pl.BlockSpec(memory_space=pltpu.VMEM)
    xh = pltpu.VMEM((slots, comps * nch, LANES), f32)
    yh = pltpu.VMEM((slots, comps * nx, LANES), f32)
    result = pl.pallas_call(
        functools.partial(kernel, ngx, ngy, comps, nx, nch, nwells, steps),
        out_shape=jax.ShapeDtypeStruct((steps, comps, rows, LANES), f32),
        in_specs=[any_spec] * 12,
        out_specs=vmem,
        scratch_shapes=[
            pltpu.VMEM(big[0].shape, f32),
            pltpu.VMEM(big[1].shape, f32),
            pltpu.VMEM(big[2].shape, big[2].dtype),
            pltpu.VMEM(big2[0].shape, f32),
            pltpu.VMEM(big2[1].shape, f32),
            pltpu.VMEM(big2[2].shape, f32),
            pltpu.VMEM(big2[3].shape, f32),
            pltpu.SMEM(delta_index.shape, jnp.int32),
            pltpu.VMEM((1, nwells), f32),
            pltpu.VMEM((1, 1, nperf), jnp.int32),
            pltpu.VMEM((1, 1, nperf), jnp.int32),
            pltpu.VMEM((steps, 2, comps, nperf), f32),
            pltpu.VMEM((BATCH, comps * rows, LANES), f32),
            pltpu.VMEM((2, comps * rows, LANES), f32),
            xh,
            xh,
            yh,
            yh,
            xh,
            xh,
            yh,
            yh,
            pltpu.VMEM((gy_rounds, ngy, 8, LANES), f32),
            pltpu.VMEM((gx_rounds, ngx, 8, LANES), f32),
            pltpu.SemaphoreType.DMA((12,)),
            pltpu.SemaphoreType.DMA((6,)),
            pltpu.SemaphoreType.DMA((slots,)),
            pltpu.SemaphoreType.DMA((slots,)),
            pltpu.SemaphoreType.DMA((slots,)),
            pltpu.SemaphoreType.DMA((slots,)),
            pltpu.SemaphoreType.DMA((gy_rounds,)),
            pltpu.SemaphoreType.DMA((gx_rounds,)),
        ],
        compiler_params=pltpu.CompilerParams(
            collective_id=0, has_side_effects=True, vmem_limit_bytes=60 * 1024 * 1024
        ),
    )(
        big[0],
        big[1],
        big[2],
        delta_index,
        big2[0],
        big2[1],
        big2[2],
        big2[3],
        well_diag.reshape(1, nwells),
        perf_well.reshape(1, 1, nperf),
        perf_cell.reshape(1, 1, nperf),
        perf_coef.reshape(steps, 2, comps, nperf),
    )
    result = result.reshape(steps, comps, nch, nx, LANES)
    return jnp.swapaxes(result, -3, -2).reshape(steps, comps, nx, ny)


def solution(mesh):
    ngx, ngy = mesh.shape["gx"], mesh.shape["gy"]
    return jax.shard_map(
        functools.partial(local, ngx, ngy),
        mesh=mesh,
        in_specs=(
            P(None, "gx", "gy"),
            P(None, "gx", "gy"),
            P(None, None, "gx", "gy"),
            P(),
            P(None, None, None, "gx", "gy"),
            P(None, None, "gx", "gy"),
            P(None, None, None, "gx", "gy"),
            P(None, "gx", "gy"),
            P("gx"),
            P("gx", "gy", None),
            P("gx", "gy", None),
            P(None, None, None, "gx", "gy", None),
        ),
        out_specs=P(None, None, "gx", "gy"),
        check_vma=False,
    )
```

time: 82.1 us -> 52.4 us (0.64)
  Pallas kernels: 72.1 us -> 50.7 us
  local copies, waits for them, and re-layouts: 9.46 us -> 1.57 us
    pallas_call x1, Pallas kernels: 72.1 us -> 50.7 us  [local(): pl.pallas_call(functools.partial(kernel, ngx, ngy, comps, nx, nch, nwells...]
    unnamed x23 -> x1, local copies, waits for them, and re-layouts: 8.77 us -> 1.57 us
where the time goes in v2:
time: 52.4 us; the launch traced here: 52.2 us
  Pallas kernels  50.7 us (97%)
  local copies, waits for them, and re-layouts  1.57 us (3%)
    pallas_call x1, Pallas kernels, local(): pl.pallas_call(functools.partial(kernel, ngx, ngy, comps, nx, nch, nwells...  50.7 us
    unnamed x1, local copies, waits for them, and re-layouts  1.57 us

profile of v2, /device:TPU:0, one launch (start us, length us, event | category | flops | bytes accessed | tf_op | source)
XLA Modules:
  0.0 52.2 jit_solution(13937083243893675178)
XLA Ops:
  0.0 50.7 %shard_map.118 = f32[2,8,16,128]{3,2,1,0:T(8,128)} custom-call(f32[8,16,128]{2,1,0:T(8,128)} %bitcast.47, f32[8,16,128]{2,1,0:T(8,128)} %bitcast.48, bf16[8,8,16,128]{3,2,1,0:T(8,128)(2,1)} %bitcast.46, s32[2,8]{1,0:T(2,128)} %index_hbm.1, f32[2,8,8,16,128]{4,3,2,1,0:T(8,128)} %bitcast.42, f32[8,8,16,128]{3,2,1,0:T(8,128)} %bitcast.43, ...), custom_call_target="tpu_custom_call" | custom-call | tf_op jit(solution)/shard_map/pallas_call | solution.py:469
  50.7 1.6 %copy.22 = f32[2,8,4,512]{3,2,1,0:T(4,128)} copy(f32[2,8,4,512]{3,2,1,0:T(4,128)} %bitcast.45) | data formatting | bytes 262144

commit v3 on v2

--- a/solution.py
+++ b/solution.py
@@ -89,6 +89,16 @@
     has_xlo, has_xhi = mx > 0, mx < ngx - 1
     has_ylo, has_yhi = my > 0, my < ngy - 1
 
+    barrier = pltpu.get_barrier_semaphore()
+    for d in range(1, ngx):
+        pl.semaphore_signal(
+            barrier, inc=1, device_id=(lax.rem(mx + d, ngx), my), device_id_type=MESH
+        )
+    for d in range(1, ngy):
+        pl.semaphore_signal(
+            barrier, inc=1, device_id=(mx, lax.rem(my + d, ngy)), device_id_type=MESH
+        )
+
     loads = []
     order = (
         (pcell_hbm, pcell_ref),
@@ -109,16 +119,6 @@
         cp.start()
         loads.append(cp)
 
-    barrier = pltpu.get_barrier_semaphore()
-    for d in range(1, ngx):
-        pl.semaphore_signal(
-            barrier, inc=1, device_id=(lax.rem(mx + d, ngx), my), device_id_type=MESH
-        )
-    for d in range(1, ngy):
-        pl.semaphore_signal(
-            barrier, inc=1, device_id=(mx, lax.rem(my + d, ngy)), device_id_type=MESH
-        )
-
     @pl.when(jnp.logical_not(has_xlo))
     def _():
         xlo_in[...] = jnp.zeros_like(xlo_in)
@@ -196,7 +196,10 @@
             part = picked[n * comps * rows : (n + 1) * comps * rows]
             part = jnp.sum(row_w * part, axis=0, keepdims=True)
             weighted = jnp.where(sub_ids == n, part, weighted)
-        start_gy(rnd, add_grams(exact_dot(weighted, well_sel, transposed=True), grams))
+        message = add_grams(exact_dot(weighted, well_sel, transposed=True), grams)
+        if rnd == 0:
+            pl.semaphore_wait(barrier, ngx + ngy - 2)
+        start_gy(rnd, message)
         kept = []
         for slot, v in zip(slots, vs):
             kept.append(send_halos(k, slot, v))
@@ -359,8 +362,6 @@
     for n in (8, 9, 10, 11):
         loads[n].wait()
 
-    pl.semaphore_wait(barrier, ngx + ngy - 2)
-
     gy_rnd = gx_rnd = slot = 0
     late = None
     for k in range(steps - 1, -1, -1):
@@ -371,20 +372,26 @@
             u0 = apply_precond(v0)
             (v1,) = operator(k, gy_rnd, [slot], [u0], row_w, col_w, None, None)
             slot += 1
+            u1 = apply_precond(v1)
+            (v2,) = operator(k, gy_rnd + 1, [slot], [u1], row_w, col_w, None, None)
         else:
             grams, part, p0, p1 = late
             starts = [v0 + accum[...] * part, accum[...] * p0, accum[...] * p1]
             firsts = [apply_precond(v) for v in starts]
             slots = [slot + n for n in range(BATCH)]
             images = operator(k, gy_rnd, slots, firsts, row_w, col_w, grams, gx_rnd)
-            slot += BATCH
+            seconds = [apply_precond(v) for v in images]
+            slots = [slot + BATCH + n for n in range(BATCH)]
+            later = operator(k, gy_rnd + 1, slots, seconds, row_w, col_w, None, None)
+            slot += 2 * BATCH - 1
             both, prod = end_gx(gx_rnd)
             gx_rnd += 1
             out_ref[k + 1] = part + both * p0 - prod * p1
-            v0, u0, v1 = (a + both * b - prod * c for a, b, c in (starts, firsts, images))
+            v0, u0, v1, u1, v2 = (
+                a + both * b - prod * c
+                for a, b, c in (starts, firsts, images, seconds, later)
+            )
         gy_rnd += 1
-        u1 = apply_precond(v1)
-        (v2,) = operator(k, gy_rnd, [slot], [u1], row_w, col_w, None, None)
         u2 = apply_precond(v2)
         grams = grams_of(v0, v1, v2)
         (v3,) = operator(k, gy_rnd + 1, [slot + 1], [u2], row_w, col_w, grams, gx_rnd)
@@ -456,7 +463,7 @@
     steps = diag_block.shape[0]
     nwells = well_diag.shape[0]
     nperf = perf_cell.shape[-1]
-    slots = 4 + (steps - 1) * (BATCH + 3)
+    slots = 4 + (steps - 1) * (2 * BATCH + 2)
     gy_rounds = 4 * steps + 1
     gx_rounds = 2 * steps
     f32 = jnp.float32

time: 52.4 us -> 50.1 us (0.956)
  Pallas kernels: 50.7 us -> 48.4 us
    pallas_call x1, Pallas kernels: 50.7 us -> 48.4 us  [local(): pl.pallas_call(functools.partial(kernel, ngx, ngy, comps, nx, nch, nwells...]
where the time goes in v3:
time: 50.1 us; the launch traced here: 49.9 us
  Pallas kernels  48.4 us (97%)
  local copies, waits for them, and re-layouts  1.57 us (3%)
    pallas_call x1, Pallas kernels, local(): pl.pallas_call(functools.partial(kernel, ngx, ngy, comps, nx, nch, nwells...  48.4 us
    unnamed x1, local copies, waits for them, and re-layouts  1.57 us

profile of v3, /device:TPU:0, one launch (start us, length us, event | category | flops | bytes accessed | tf_op | source)
XLA Modules:
  0.0 49.9 jit_solution(12142582970019198047)
XLA Ops:
  0.0 48.4 %shard_map.118 = f32[2,8,16,128]{3,2,1,0:T(8,128)} custom-call(f32[8,16,128]{2,1,0:T(8,128)} %bitcast.47, f32[8,16,128]{2,1,0:T(8,128)} %bitcast.48, bf16[8,8,16,128]{3,2,1,0:T(8,128)(2,1)} %bitcast.46, s32[2,8]{1,0:T(2,128)} %index_hbm.1, f32[2,8,8,16,128]{4,3,2,1,0:T(8,128)} %bitcast.42, f32[8,8,16,128]{3,2,1,0:T(8,128)} %bitcast.43, ...), custom_call_target="tpu_custom_call" | custom-call | tf_op jit(solution)/shard_map/pallas_call | solution.py:476
  48.4 1.6 %copy.22 = f32[2,8,4,512]{3,2,1,0:T(4,128)} copy(f32[2,8,4,512]{3,2,1,0:T(4,128)} %bitcast.45) | data formatting | bytes 262144
